TPU v7x, 32 devices: a whole 2x2x4 slice. The times are simulated.
32 devices in a mesh: wide: 8 (over y, x, core), layer: 4 (over z).
Axes of the slice: x: 2, y: 2, z: 4, core: 2. Of those that a mesh axis runs over, the one named last changes fastest.
Arguments:
- factor: float32 [4096, 1024], P('layer', 'wide'), parts along dimension 0, may hold values from -1 to 21, as said below
Outputs:
- rotated: float32 [4096, 1024], P('layer', 'wide'), parts along dimension 0
- eigen_basis: float32 [4096, 1024], P('layer', 'wide'), parts along dimension 0
There are 4 independent parts, one for each index of `layer`. A program takes and returns all parts, laid end to end along the dimension named above; each array names one. Nothing has to cross between parts.
Inputs may be any that keep to these rules, and one draw needn't show every extreme that they name: `factor`: symmetric.
All inputs are finite; a program needn't handle non-finite values.
Results may differ from a plain program's by a relative error of at most 0.00095.
Values sent between devices are 32-bit elements; how exact they have to be, the bound alone decides.
No kernel may reach another device: no remote copies, remote signals or barrier semaphores. Data moves between devices by JAX's collectives and lax.ppermute only.
A program may use at most 128 MiB of HBM per device.

v0:
```python
import functools
import jax
import jax.numpy as jnp
from jax import lax
from jax.experimental import pallas as pl
from jax.experimental.pallas import tpu as pltpu
from jax.sharding import PartitionSpec as P

SWEEPS = 3
FLOOR = 0.01
TOLERANCE = 3e-6


def schedule(bound, steps=None, weight=1.0, goal=1e-6):
    theta = bound / (2.0 + bound)
    mus = []
    while len(mus) < steps if steps else theta > goal:
        mus.append(2.0 / (2.0 - theta * theta))
        theta = theta * theta / (2.0 - theta * theta)
    return 1.0 / (1.0 + 0.5 * bound), tuple(mus), weight


def split(x):
    high = x.astype(jnp.bfloat16)
    x = x - high.astype(jnp.float32)
    middle = x.astype(jnp.bfloat16)
    return high, middle, (x - middle.astype(jnp.float32)).astype(jnp.bfloat16)


def below(*parts):
    return tuple(jnp.concatenate(each, axis=0) for each in zip(*parts))


def product(a, b):
    a_high, a_middle, a_low = a
    b_high, b_middle, b_low = b
    n = b_high.shape[1]
    wide = jnp.concatenate([b_high, b_middle], axis=1)
    most = jnp.dot(
        jnp.concatenate([a_high, a_middle], axis=1),
        jnp.concatenate([wide, wide], axis=0),
        preferred_element_type=jnp.float32,
    )
    rest = jnp.dot(
        jnp.concatenate([a_high, a_low], axis=1),
        jnp.concatenate([b_low, b_high], axis=0),
        preferred_element_type=jnp.float32,
    )
    return most[:, :n] + (most[:, n:] + rest)


def exact(a, b):
    return jnp.dot(a, b, precision=lax.Precision.HIGHEST, preferred_element_type=jnp.float32)


def identity_of(n):
    row = lax.broadcasted_iota(jnp.int32, (n, n), 0)
    col = lax.broadcasted_iota(jnp.int32, (n, n), 1)
    return (row == col).astype(jnp.float32)


def ratios_of(m, eye):
    kept = m * eye
    spread = jnp.sum(kept, axis=0, keepdims=True) - jnp.sum(kept, axis=1, keepdims=True)
    return m * spread / (spread * spread + 2.0 * m * m + FLOOR)


def sure_sweep(m, qt, eye):
    n = m.shape[0]
    ratios = ratios_of(m, eye)
    a = 0.25 * (ratios - ratios.T)
    system = eye - exact(a, a)
    scale, mus, _ = schedule(n * n / 32.0)

    def newton(_, y):
        return y + exact(y, eye - exact(system, y))

    y = lax.fori_loop(0, len(mus) + 6, newton, scale * eye)
    x = exact(y, eye + a)
    x = x + exact(x, eye - (x - exact(a, x)))
    turn = 2.0 * x - eye
    return exact(turn.T, exact(m, turn)), exact(turn.T, qt)


def solve(blocks, plans, eye, keep):
    n = eye.shape[0]
    some = range(len(blocks))
    ms, qts = list(blocks), None
    worst = jnp.zeros((1, n), jnp.float32)
    for index, (scale, mus, weight) in enumerate(plans):
        carried = keep or index + 1 < len(plans)
        skews = [0.5 * ratios_of(m, eye) for m in ms]
        parts = [split(a) for a in skews]
        if carried:
            firsts = [product(below(a, split(m)), a) for a, m in zip(parts, ms)]
        else:
            firsts = [product(a, a) for a in parts]
        errors = [(1.0 - scale) * eye + scale * first[:n] for first in firsts]
        stacks = [scale * (eye - a) for a in skews]
        if carried:
            stacks = [
                jnp.concatenate([stack, scale * (m + first[n:])], axis=0)
                for stack, m, first in zip(stacks, ms, firsts)
            ]
        for mu in mus:
            parts = [split(error) for error in errors]
            if len(parts) == 1:
                squares = [product(part, part) for part in parts]
                steps = [product(split(stack), part) for part, stack in zip(parts, stacks)]
            else:
                both = [product(below(part, split(stack)), part) for part, stack in zip(parts, stacks)]
                squares, steps = [each[:n] for each in both], [each[n:] for each in both]
            errors = [(1.0 - mu) * eye + mu * square for square in squares]
            stacks = [mu * (stack + step) for stack, step in zip(stacks, steps)]
        for error in errors:
            worst = worst + weight * jnp.sum(error * error, axis=0, keepdims=True)
        backs = [2.0 * stack[:n] - eye for stack in stacks]
        rights = [[] for _ in some]
        if carried:
            rights = [[2.0 * stack[n:] - m] for stack, m in zip(stacks, ms)]
        if qts is not None:
            rights = [right + [qt] for right, qt in zip(rights, qts)]
        turned = [
            product(split(back), split(jnp.concatenate(right, axis=1)))
            for back, right in zip(backs, rights)
        ]
        qts = backs if qts is None else [both[:, -n:] for both in turned]
        if carried:
            ms = [both[:, :n] for both in turned]
    return ms, qts, worst


def settled(worst):
    return jnp.sum(worst) <= TOLERANCE * TOLERANCE * worst.shape[1]


def solve_surely(blocks, m_ref, qt_ref, eye):
    for k in range(len(blocks)):
        m_ref[k] = blocks[k]
        qt_ref[k] = eye

    def again(step, carry):
        k = step // SWEEPS
        m_ref[k], qt_ref[k] = sure_sweep(m_ref[k], qt_ref[k], eye)
        return carry

    lax.fori_loop(0, SWEEPS * len(blocks), again, 0)


PLANS = (
    (schedule(4.0, 4), schedule(3.0, 4), schedule(0.95, 3)),
    (schedule(0.8, 3), schedule(0.5, 3), schedule(0.2, 2, 0.01)),
)


def halves(x):
    high = x.astype(jnp.bfloat16)
    return high, (x - high.astype(jnp.float32)).astype(jnp.bfloat16)


def quick(a, b):
    n = b.shape[1]
    wide = jnp.concatenate(halves(b), axis=1)
    both = jnp.dot(
        jnp.concatenate(halves(a), axis=1),
        jnp.concatenate([wide, wide], axis=0),
        preferred_element_type=jnp.float32,
    )
    return both[:, :n] + both[:, n:]


def pair_up(first, last, corner):
    n = first.shape[0]
    row = lax.broadcasted_iota(jnp.int32, (n, n), 0) < n // 2
    col = lax.broadcasted_iota(jnp.int32, (n, n), 1) < n // 2
    return jnp.where(row == col, jnp.where(row, first, last), corner + corner.T)


def rows_of(pair, n):
    return pl.ds(pl.multiple_of(pair * n, n), n)


def first_kernel(own_ref, packed_ref, qt_ref, m_ref):
    n = own_ref.shape[0]
    half = n // 2
    eye = identity_of(n)
    col = lax.broadcasted_iota(jnp.int32, (half, n), 1) < half

    def finish(m, qt):
        packed_ref[:n, :] = qt
        packed_ref[n:, :] = jnp.where(col, m[:half], m[half:])

    (m,), (qt,), worst = solve([own_ref[...]], PLANS[0], eye, True)
    qt_ref[0] = qt
    m_ref[0] = m
    finish(m, qt)

    @pl.when(jnp.logical_not(settled(worst)))
    def _():
        solve_surely([own_ref[...]], m_ref, qt_ref, eye)
        finish(m_ref[0], qt_ref[0])


def columns_kernel(factor_ref, cross_ref, qt_ref, columns_ref, right_ref, moved_ref):
    order_size, n = factor_ref.shape
    half, middle = n // 2, order_size // 2
    turn = qt_ref[0].T
    moved_ref[...] = product(split(cross_ref[...]), split(turn))
    for start in range(0, middle, n):
        upper = quick(factor_ref[start : start + n, :], turn)
        lower = quick(factor_ref[middle + start : middle + start + n, :], turn)
        columns_ref[start : start + n, :] = upper
        columns_ref[middle + start : middle + start + n, :] = lower
        right_ref[start : start + n, :] = jnp.concatenate([upper[:, half:], lower[:, half:]], axis=1)


def second_kernel(packed_ref, m_in_ref, own_ref, moved_ref, second_ref, first_ref, block_ref, m_ref):
    n = moved_ref.shape[0]
    eye = identity_of(n)
    qt, packed = packed_ref[:n, :], packed_ref[n:, :]
    first_ref[0] = own_ref[0]
    first_ref[1] = qt
    cross = product(split(qt), split(moved_ref[...]))
    own, partner = m_in_ref[0], jnp.concatenate([packed, packed], axis=0)
    row = lax.broadcasted_iota(jnp.int32, (n, n), 0) < n // 2
    col = lax.broadcasted_iota(jnp.int32, (n, n), 1) < n // 2
    lower = jnp.where(jnp.logical_and(jnp.logical_not(row), col), cross, 0.0)
    upper = jnp.where(jnp.logical_and(row, jnp.logical_not(col)), cross, 0.0)
    blocks = [pair_up(own, partner, lower), pair_up(partner, own, upper)]
    block_ref[0], block_ref[1] = blocks
    _, (second_ref[0], second_ref[1]), worst = solve(blocks, PLANS[1], eye, False)

    @pl.when(jnp.logical_not(settled(worst)))
    def _():
        solve_surely([block_ref[0], block_ref[1]], m_ref, second_ref, eye)


def turn_kernel(far, columns_ref, second_ref, first_ref, turned_ref, turn_ref, out_ref):
    order_size, n = columns_ref.shape
    half = n // 2
    me = lax.axis_index("wide")
    row = lax.broadcasted_iota(jnp.int32, (n, n), 0) < half
    turn = second_ref[0].T
    turn_ref[...] = turn
    out_ref[...] = jnp.zeros_like(out_ref)
    out_ref[rows_of(me, n), :] = quick(jnp.where(row, first_ref[0], 0.0).T, turn)
    out_ref[rows_of(me ^ far, n), :] = quick(jnp.where(row, 0.0, first_ref[1]).T, turn)
    upper = jnp.where(row, turn, 0.0)
    for start in range(0, order_size, n):
        turned_ref[start : start + n, :] = quick(columns_ref[start : start + n, :], upper)


def trade_kernel(masks, far, turned_ref, turn_ref, right_ref, *refs):
    refs, mixed_ref, whole_ref = refs[:-2], refs[-2], refs[-1]
    order_size, n = turned_ref.shape
    half, middle = n // 2, order_size // 2
    me = lax.axis_index("wide")
    row = lax.broadcasted_iota(jnp.int32, (n, n), 0) < half
    turn = turn_ref[...]
    first = jnp.where(row, jnp.concatenate([turn[half:], turn[half:]], axis=0), 0.0)
    last = jnp.where(row, 0.0, turn)
    for start in range(0, middle, n):
        upper, lower = slice(start, start + n), slice(middle + start, middle + start + n)
        whole_ref[upper, :] = turned_ref[upper, :] + quick(right_ref[upper, :], first)
        whole_ref[lower, :] = turned_ref[lower, :] + quick(right_ref[upper, :], last)
    for mask, (near_ref, away_ref) in zip(masks, two_by_two(refs)):
        pair, other = rows_of(me ^ mask, n), rows_of(me ^ mask ^ far, n)
        near = quick(near_ref[...], whole_ref[pair, :])
        away = quick(away_ref[...], whole_ref[other, :])
        mixed_ref[pair, :] = jnp.concatenate([near[:half], away[half:]], axis=0)
        mixed_ref[other, :] = jnp.concatenate([away[:half], near[half:]], axis=0)


def two_by_two(refs):
    couples, held = [], []
    for ref in refs:
        held += [ref.at[side] for side in range(ref.shape[0])]
        if len(held) == 2:
            couples.append(held)
            held = []
    return couples


def rows_kernel(masks, far, mixed_ref, *refs):
    refs, out_ref = refs[:-1], refs[-1]
    n = mixed_ref.shape[1]
    me = lax.axis_index("wide")
    for mask, turn_ref in zip(masks, refs):
        for side in range(2):
            rows = rows_of(me ^ mask ^ (far * side), n)
            out_ref[rows, :] = quick(turn_ref[side], mixed_ref[rows, :])


def last_rows_kernel(masks, far, mixed_ref, *refs):
    turn_refs, (_, out_ref, block_ref, sem_ref) = refs[:-4], refs[-4:]
    n = mixed_ref.shape[1]
    me = lax.axis_index("wide")
    copies = []
    for mask, turn_ref in zip(masks, turn_refs):
        for side in range(2):
            rows = rows_of(me ^ mask ^ (far * side), n)
            place = len(copies)
            block_ref[place] = quick(turn_ref[side], mixed_ref[rows, :])
            copy = pltpu.make_async_copy(block_ref.at[place], out_ref.at[rows, :], sem_ref.at[place])
            copy.start()
            copies.append(copy)
    for copy in copies:
        copy.wait()


def call(kernel, out_shape, scratch_shapes, flops, *args, **more):
    return pl.pallas_call(
        kernel,
        out_shape=out_shape,
        scratch_shapes=scratch_shapes,
        compiler_params=pltpu.CompilerParams(vmem_limit_bytes=48 * 1024 * 1024),
        cost_estimate=pl.CostEstimate(flops=flops, bytes_accessed=2**20, transcendentals=0),
        **more,
    )(*args)


def swap(shard, mask):
    return lax.ppermute(shard, "wide", [(i, i ^ mask) for i in range(lax.axis_size("wide"))])


def after(value, gate):
    return lax.optimization_barrier((value, gate))[0]


def spread_first(own, early, both, far, gate):
    pieces = [(0, (both,))]
    if early:
        pieces.append((far // 2, early))
    bit = far // 4
    while bit:
        pieces += [
            (mask | bit, tuple(swap(after(held, gate), bit) for held in couple))
            for mask, couple in pieces
        ]
        bit //= 2
    return [mask for mask, _ in pieces], [held for _, couple in pieces for held in couple]


def spread_second(both, far, gate):
    pieces = [(0, both)]
    bit = far // 2
    while bit:
        pieces += [
            (mask | bit, swap(after(held, gate) if mask and bit == 1 else held, bit))
            for mask, held in pieces
        ]
        bit //= 2
    return pieces


def body(factor):
    far = lax.axis_size("wide") // 2
    me = lax.axis_index("wide")
    order_size, n = factor.shape

    def like(*shape):
        return jax.ShapeDtypeStruct(shape, jnp.float32)

    one, two, tall = like(1, n, n), like(2, n, n), like(order_size, n)
    own = lax.dynamic_slice_in_dim(factor, me * n, n, 0)
    cross = lax.dynamic_slice_in_dim(factor, (me ^ far) * n, n, 0)
    packed, qt, m = call(first_kernel, (like(n + n // 2, n), one, one), [], 2**32, own)
    packed = swap(packed, far)
    early = (swap(qt, far // 2), swap(qt, far // 2 | far)) if far > 1 else ()
    columns, right, moved = call(
        columns_kernel, (tall, like(order_size // 2, n), like(n, n)), [], 2**28, factor, cross, qt
    )
    right = swap(right, far)
    scratch = [pltpu.VMEM((2, n, n), jnp.float32)] * 2
    second, both = call(second_kernel, (two, two), scratch, 2**34, packed, m, qt, moved)
    masks, firsts = spread_first(qt, early, both, far, second)
    turned, turn, eigen_basis = call(
        functools.partial(turn_kernel, far),
        (tall, like(n, n), tall),
        [],
        2**31,
        columns,
        second,
        both,
    )
    mixed = call(
        functools.partial(trade_kernel, masks, far),
        tall,
        [pltpu.VMEM((order_size, n), jnp.float32)],
        2**31,
        turned,
        turn,
        right,
        *firsts,
    )
    pieces = spread_second(second, far, mixed)
    soon = [piece for piece in pieces if piece[0] < 2 or not piece[0] & 1]
    late = [piece for piece in pieces if piece[0] >= 2 and piece[0] & 1]
    masks, held = zip(*soon)
    rotated = call(functools.partial(rows_kernel, masks, far), tall, [], 2**29, mixed, *held)
    if late:
        masks, held = zip(*late)
        anywhere = pl.BlockSpec(memory_space=pl.ANY)
        inside = pl.BlockSpec(memory_space=pltpu.VMEM)
        rotated = call(
            functools.partial(last_rows_kernel, masks, far),
            tall,
            [
                pltpu.VMEM((2 * len(late), n, n), jnp.float32),
                pltpu.SemaphoreType.DMA((2 * len(late),)),
            ],
            2**29,
            mixed,
            *held,
            rotated,
            in_specs=[inside] * (1 + len(late)) + [anywhere],
            out_specs=anywhere,
            input_output_aliases={1 + len(late): 0},
        )
    return (rotated, eigen_basis)


def solution(mesh):
    return jax.shard_map(
        body,
        mesh=mesh,
        in_specs=(P("layer", "wide"),),
        out_specs=(P("layer", "wide"), P("layer", "wide")),
        check_vma=False,
    )
```

profile of v0, /device:TPU:9, one launch (start us, length us, event | category | flops | bytes accessed | tf_op | source)
XLA Modules:
  0.0 45.2 jit_solution(1012301128820778229)
XLA Ops:
  0.6 0.9 %constant_dynamic-slice_fusion = (f32[128,128]{1,0:T(8,128)S(1)}, f32[128,128]{1,0:T(8,128)S(1)}) fusion(f32[1024,128]{1,0:T(8,128)} %factor_ref.1, s32[]{:T(128)S(6)} %select_n.7, s32[]{:T(128)S(6)} %select_n.6), kind=kLoop, calls=%fused_computation | loop fusion | bytes 262152 | tf_op jit(solution)/shard_map/dynamic_slice | solution.py:365
  1.5 0.0 copy-start
  1.5 3.8 %shard_map.30 = (f32[192,128]{1,0:T(8,128)S(1)}, f32[1,128,128]{2,1,0:T(8,128)S(1)}, f32[1,128,128]{2,1,0:T(8,128)S(1)}) custom-call(f32[128,128]{1,0:T(8,128)S(1)} %get-tuple-element.32.own_ref), custom_call_target="tpu_custom_call" | custom-call | flops 4294967296 | bytes 1048576 | tf_op jit(solution)/shard_map/pallas_call | solution.py:312
  5.4 1.3 %collective-permute-start = (f32[192,128]{1,0:T(8,128)S(1)}, f32[192,128]{1,0:T(8,128)S(1)}, u32[]{:S(2)}, u32[]{:S(2)}) collective-permute-start(f32[192,128]{1,0:T(8,128)S(1)} %get-tuple-element.19), channel_id=1, source_target_pairs={{0,16},{4,20},{8,24},{12,28},{16,0},{20,4},{24,8},{28,12},{1,17},{... | collective-permute-start | bytes 294920 | tf_op jit(solution)/shard_map/ppermute | solution.py:323
  6.7 1.2 %collective-permute-start.2 = (f32[1,128,128]{2,1,0:T(8,128)S(1)}, f32[1,128,128]{2,1,0:T(8,128)S(1)}, u32[]{:S(2)}, u32[]{:S(2)}) collective-permute-start(f32[1,128,128]{2,1,0:T(8,128)S(1)} %get-tuple-element.17.qt_ref.own_ref), channel_id=1, source_target_pairs={{0,8},{4,12},{8,0},{12,4},{16,24},{20,28},{24,16},{28,20},{1,9},{5... | collective-permute-start | bytes 196616 | tf_op jit(solution)/shard_map/ppermute | solution.py:323
  7.9 0.2 collective-permute-start.3
  8.1 0.0 copy-done
  8.1 0.5 %shard_map.31 = (f32[1024,128]{1,0:T(8,128)S(1)}, f32[512,128]{1,0:T(8,128)S(1)}, f32[128,128]{1,0:T(8,128)S(1)}) custom-call(f32[1024,128]{1,0:T(8,128)S(1)} %copy-done, f32[128,128]{1,0:T(8,128)S(1)} %get-tuple-element.33.cross_ref, f32[1,128,128]{2,1,0:T(8,128)S(1)} %get-tuple-element.17.qt_ref.own_ref), custom_call_target="tpu_custom_call" | custom-call | flops 268435456 | bytes 1048576 | tf_op jit(solution)/shard_map/pallas_call | solution.py:312
  8.6 1.3 %collective-permute-start.1 = (f32[512,128]{1,0:T(8,128)S(1)}, f32[512,128]{1,0:T(8,128)S(1)}, u32[]{:S(2)}, u32[]{:S(2)}) collective-permute-start(f32[512,128]{1,0:T(8,128)S(1)} %get-tuple-element.26), channel_id=1, source_target_pairs={{0,16},{4,20},{8,24},{12,28},{16,0},{20,4},{24,8},{28,12},{1,17},{... | collective-permute-start | bytes 786440 | tf_op jit(solution)/shard_map/ppermute | solution.py:323
  9.9 0.0 collective-permute-done.packed_ref
  9.9 3.5 %shard_map.32 = (f32[2,128,128]{2,1,0:T(8,128)S(1)}, f32[2,128,128]{2,1,0:T(8,128)S(1)}) custom-call(f32[192,128]{1,0:T(8,128)S(1)} %collective-permute-done.packed_ref, f32[1,128,128]{2,1,0:T(8,128)S(1)} %get-tuple-element.20.m_in_ref, f32[1,128,128]{2,1,0:T(8,128)S(1)} %get-tuple-element.17.qt_ref.own_ref, f32[128,128]{1,0:T(8,128)S(1)} %get-tuple-element.21.moved_ref), custom_call_target="tpu_custom_call" | custom-call | flops 17179869184 | bytes 1048576 | tf_op jit(solution)/shard_map/pallas_call | solution.py:312
  13.4 1.3 %collective-permute-start.7 = (f32[2,128,128]{2,1,0:T(8,128)S(1)}, f32[2,128,128]{2,1,0:T(8,128)S(1)}, u32[]{:S(2)}, u32[]{:S(2)}) collective-permute-start(f32[2,128,128]{2,1,0:T(8,128)S(1)} %get-tuple-element.22.second_ref.refs_0_), channel_id=1, source_target_pairs={{0,8},{4,12},{8,0},{12,4},{16,24},{20,28},{24,16},{28,20},{1,9},{5... | collective-permute-start | bytes 393224 | tf_op jit(solution)/shard_map/ppermute | solution.py:323
  14.7 25.6 %collective-permute-start.4 = (f32[2,128,128]{2,1,0:T(8,128)S(1)}, f32[2,128,128]{2,1,0:T(8,128)S(1)}, u32[]{:S(2)}, u32[]{:S(2)}) collective-permute-start(f32[2,128,128]{2,1,0:T(8,128)S(1)} %get-tuple-element.27.first_ref.refs_0_), channel_id=1, source_target_pairs={{0,4},{4,0},{8,12},{12,8},{16,20},{20,16},{24,28},{28,24},{1,5},{5... | collective-permute-start | bytes 393224 | tf_op jit(solution)/shard_map/ppermute | solution.py:323
  40.3 0.0 collective-permute-done.2.refs_1_
  40.3 0.0 collective-permute-start.5
  40.3 0.0 collective-permute-done.3.refs_2_
  40.3 0.5 %collective-permute-start.6 = (f32[1,128,128]{2,1,0:T(8,128)S(1)}, f32[1,128,128]{2,1,0:T(8,128)S(1)}, u32[]{:S(2)}, u32[]{:S(2)}) collective-permute-start(f32[1,128,128]{2,1,0:T(8,128)S(1)} %collective-permute-done.3.refs_2_), channel_id=1, source_target_pairs={{0,4},{4,0},{8,12},{12,8},{16,20},{20,16},{24,28},{28,24},{1,5},{5... | collective-permute-start | bytes 196616 | tf_op jit(solution)/shard_map/ppermute | solution.py:323
  40.8 1.1 %shard_map.33 = (f32[1024,128]{1,0:T(8,128)S(1)}, f32[128,128]{1,0:T(8,128)S(1)}, f32[1024,128]{1,0:T(8,128)}) custom-call(f32[1024,128]{1,0:T(8,128)S(1)} %get-tuple-element.18.columns_ref, f32[2,128,128]{2,1,0:T(8,128)S(1)} %get-tuple-element.22.second_ref.refs_0_, f32[2,128,128]{2,1,0:T(8,128)S(1)} %get-tuple-element.27.first_ref.refs_0_), custom_call_target="tpu_custom_call" | custom-call | flops 2147483648 | bytes 1048576 | tf_op jit(solution)/shard_map/pallas_call | solution.py:312
  41.9 0.0 collective-permute-done.5.refs_4_
  42.0 0.1 collective-permute-start.9
  42.0 0.0 collective-permute-done.6.refs_5_
  42.0 0.0 collective-permute-done.4.refs_3_
  42.0 0.0 collective-permute-done.1.right_ref
  42.0 0.6 %shard_map.34.mixed_ref = f32[1024,128]{1,0:T(8,128)S(1)} custom-call(f32[1024,128]{1,0:T(8,128)S(1)} %get-tuple-element.24.turned_ref, f32[128,128]{1,0:T(8,128)S(1)} %get-tuple-element.25.turn_ref, f32[512,128]{1,0:T(8,128)S(1)} %collective-permute-done.1.right_ref, f32[2,128,128]{2,1,0:T(8,128)S(1)} %get-tuple-element.27.first_ref.refs_0_, ...), custom_call_target="tpu_custom_call" | custom-call | flops 2147483648 | bytes 1048576 | tf_op jit(solution)/shard_map/pallas_call | solution.py:312
  42.7 0.0 collective-permute-done.7.refs_1_
  42.7 0.6 %collective-permute-start.8 = (f32[2,128,128]{2,1,0:T(8,128)S(1)}, f32[2,128,128]{2,1,0:T(8,128)S(1)}, u32[]{:S(2)}, u32[]{:S(2)}) collective-permute-start(f32[2,128,128]{2,1,0:T(8,128)S(1)} %collective-permute-done.7.refs_1_), channel_id=1, source_target_pairs={{0,4},{4,0},{8,12},{12,8},{16,20},{20,16},{24,28},{28,24},{1,5},{5... | collective-permute-start | bytes 393224 | tf_op jit(solution)/shard_map/ppermute | solution.py:323
  43.3 0.0 collective-permute-done.9.refs_2_
  43.3 1.1 %shard_map.35.refs_1_ = f32[1024,128]{1,0:T(8,128)} custom-call(f32[1024,128]{1,0:T(8,128)S(1)} %shard_map.34.mixed_ref, f32[2,128,128]{2,1,0:T(8,128)S(1)} %get-tuple-element.22.second_ref.refs_0_, f32[2,128,128]{2,1,0:T(8,128)S(1)} %collective-permute-done.7.refs_1_, f32[2,128,128]{2,1,0:T(8,128)S(1)} %collective-permute-done.9.refs_2_), custom_call_target="tpu_custom_call" | custom-call | flops 536870912 | bytes 1048576 | tf_op jit(solution)/shard_map/pallas_call | solution.py:312
  44.4 0.0 collective-permute-done.8.refs_0_
  44.4 0.9 %shard_map.36 = f32[1024,128]{1,0:T(8,128)} custom-call(f32[1024,128]{1,0:T(8,128)S(1)} %shard_map.34.mixed_ref, f32[2,128,128]{2,1,0:T(8,128)S(1)} %collective-permute-done.8.refs_0_, f32[1024,128]{1,0:T(8,128)} %shard_map.35.refs_1_), custom_call_target="tpu_custom_call", output_to_operand_aliasing={{}: (2, {})} | custom-call | flops 536870912 | bytes 1048576 | tf_op jit(solution)/shard_map/pallas_call | solution.py:312
Async XLA Ops:
  1.5 6.6 %copy-start = (f32[1024,128]{1,0:T(8,128)S(1)}, f32[1024,128]{1,0:T(8,128)}, u32[]{:S(2)}) copy-start(f32[1024,128]{1,0:T(8,128)} %factor_ref.1) | copy-start | bytes 1572868
  5.4 4.5 %collective-permute-start = (f32[192,128]{1,0:T(8,128)S(1)}, f32[192,128]{1,0:T(8,128)S(1)}, u32[]{:S(2)}, u32[]{:S(2)}) collective-permute-start(f32[192,128]{1,0:T(8,128)S(1)} %get-tuple-element.19), channel_id=1, source_target_pairs={{0,16},{4,20},{8,24},{12,28},{16,0},{20,4},{24,8},{28,12},{1,17},{... | collective-permute-start | bytes 294920 | tf_op jit(solution)/shard_map/ppermute | solution.py:323
  6.7 33.6 %collective-permute-start.2 = (f32[1,128,128]{2,1,0:T(8,128)S(1)}, f32[1,128,128]{2,1,0:T(8,128)S(1)}, u32[]{:S(2)}, u32[]{:S(2)}) collective-permute-start(f32[1,128,128]{2,1,0:T(8,128)S(1)} %get-tuple-element.17.qt_ref.own_ref), channel_id=1, source_target_pairs={{0,8},{4,12},{8,0},{12,4},{16,24},{20,28},{24,16},{28,20},{1,9},{5... | collective-permute-start | bytes 196616 | tf_op jit(solution)/shard_map/ppermute | solution.py:323
  7.9 32.4 %collective-permute-start.3 = (f32[1,128,128]{2,1,0:T(8,128)S(1)}, f32[1,128,128]{2,1,0:T(8,128)S(1)}, u32[]{:S(2)}, u32[]{:S(2)}) collective-permute-start(f32[1,128,128]{2,1,0:T(8,128)S(1)} %get-tuple-element.17.qt_ref.own_ref), channel_id=1, source_target_pairs={{0,24},{4,28},{8,16},{12,20},{16,8},{20,12},{24,0},{28,4},{1,25},{... | collective-permute-start | bytes 196616 | tf_op jit(solution)/shard_map/ppermute | solution.py:323
  8.6 33.5 %collective-permute-start.1 = (f32[512,128]{1,0:T(8,128)S(1)}, f32[512,128]{1,0:T(8,128)S(1)}, u32[]{:S(2)}, u32[]{:S(2)}) collective-permute-start(f32[512,128]{1,0:T(8,128)S(1)} %get-tuple-element.26), channel_id=1, source_target_pairs={{0,16},{4,20},{8,24},{12,28},{16,0},{20,4},{24,8},{28,12},{1,17},{... | collective-permute-start | bytes 786440 | tf_op jit(solution)/shard_map/ppermute | solution.py:323
  13.4 29.3 %collective-permute-start.7 = (f32[2,128,128]{2,1,0:T(8,128)S(1)}, f32[2,128,128]{2,1,0:T(8,128)S(1)}, u32[]{:S(2)}, u32[]{:S(2)}) collective-permute-start(f32[2,128,128]{2,1,0:T(8,128)S(1)} %get-tuple-element.22.second_ref.refs_0_), channel_id=1, source_target_pairs={{0,8},{4,12},{8,0},{12,4},{16,24},{20,28},{24,16},{28,20},{1,9},{5... | collective-permute-start | bytes 393224 | tf_op jit(solution)/shard_map/ppermute | solution.py:323
  14.7 27.3 %collective-permute-start.4 = (f32[2,128,128]{2,1,0:T(8,128)S(1)}, f32[2,128,128]{2,1,0:T(8,128)S(1)}, u32[]{:S(2)}, u32[]{:S(2)}) collective-permute-start(f32[2,128,128]{2,1,0:T(8,128)S(1)} %get-tuple-element.27.first_ref.refs_0_), channel_id=1, source_target_pairs={{0,4},{4,0},{8,12},{12,8},{16,20},{20,16},{24,28},{28,24},{1,5},{5... | collective-permute-start | bytes 393224 | tf_op jit(solution)/shard_map/ppermute | solution.py:323
  40.3 1.6 %collective-permute-start.5 = (f32[1,128,128]{2,1,0:T(8,128)S(1)}, f32[1,128,128]{2,1,0:T(8,128)S(1)}, u32[]{:S(2)}, u32[]{:S(2)}) collective-permute-start(f32[1,128,128]{2,1,0:T(8,128)S(1)} %collective-permute-done.2.refs_1_), channel_id=1, source_target_pairs={{0,4},{4,0},{8,12},{12,8},{16,20},{20,16},{24,28},{28,24},{1,5},{5... | collective-permute-start | bytes 196616 | tf_op jit(solution)/shard_map/ppermute | solution.py:323
  40.3 1.7 %collective-permute-start.6 = (f32[1,128,128]{2,1,0:T(8,128)S(1)}, f32[1,128,128]{2,1,0:T(8,128)S(1)}, u32[]{:S(2)}, u32[]{:S(2)}) collective-permute-start(f32[1,128,128]{2,1,0:T(8,128)S(1)} %collective-permute-done.3.refs_2_), channel_id=1, source_target_pairs={{0,4},{4,0},{8,12},{12,8},{16,20},{20,16},{24,28},{28,24},{1,5},{5... | collective-permute-start | bytes 196616 | tf_op jit(solution)/shard_map/ppermute | solution.py:323
  42.0 1.3 %collective-permute-start.9 = (f32[2,128,128]{2,1,0:T(8,128)S(1)}, f32[2,128,128]{2,1,0:T(8,128)S(1)}, u32[]{:S(2)}, u32[]{:S(2)}) collective-permute-start(f32[2,128,128]{2,1,0:T(8,128)S(1)} %get-tuple-element.22.second_ref.refs_0_), channel_id=1, source_target_pairs={{0,4},{4,0},{8,12},{12,8},{16,20},{20,16},{24,28},{28,24},{1,5},{5... | collective-permute-start | bytes 393224 | tf_op jit(solution)/shard_map/ppermute | solution.py:323
  42.7 1.7 %collective-permute-start.8 = (f32[2,128,128]{2,1,0:T(8,128)S(1)}, f32[2,128,128]{2,1,0:T(8,128)S(1)}, u32[]{:S(2)}, u32[]{:S(2)}) collective-permute-start(f32[2,128,128]{2,1,0:T(8,128)S(1)} %collective-permute-done.7.refs_1_), channel_id=1, source_target_pairs={{0,4},{4,0},{8,12},{12,8},{16,20},{20,16},{24,28},{28,24},{1,5},{5... | collective-permute-start | bytes 393224 | tf_op jit(solution)/shard_map/ppermute | solution.py:323
where the time goes:
time: 45.9 us; the launch traced here: 45.2 us
  starting transfers between devices  32 us (70%)
  Pallas kernels  11.6 us (25%)
  local copies, waits for them, and re-layouts  0.89 us (2%)
  between operations  0.69 us (2%)
    ppermute x10, starting transfers between devices, swap(): lax.ppermute(shard, 'wide', [(i, i ^ mask) for i in range(lax.axis_size('...  32 us
    pallas_call x7, Pallas kernels, call(): pl.pallas_call(kernel, out_shape=out_shape, scratch_shapes=scratch_shapes...  11.6 us
  transfers between devices with their start and end apart: 10, of which 0 were waited for; matrix products, arithmetic and copies ran while one was open for 0% of the time, Pallas kernels for 15%

commit v1 on v0

--- a/solution.py
+++ b/solution.py
@@ -201,11 +201,13 @@
         finish(m_ref[0], qt_ref[0])
 
 
-def columns_kernel(factor_ref, cross_ref, qt_ref, columns_ref, right_ref, moved_ref):
+def columns_kernel(far, factor_ref, qt_ref, columns_ref, right_ref, moved_ref):
     order_size, n = factor_ref.shape
     half, middle = n // 2, order_size // 2
     turn = qt_ref[0].T
-    moved_ref[...] = product(split(cross_ref[...]), split(turn))
+    moved_ref[...] = product(
+        split(factor_ref[rows_of(lax.axis_index("wide") ^ far, n), :]), split(turn)
+    )
     for start in range(0, middle, n):
         upper = quick(factor_ref[start : start + n, :], turn)
         lower = quick(factor_ref[middle + start : middle + start + n, :], turn)
@@ -282,17 +284,7 @@
 
 
 def rows_kernel(masks, far, mixed_ref, *refs):
-    refs, out_ref = refs[:-1], refs[-1]
-    n = mixed_ref.shape[1]
-    me = lax.axis_index("wide")
-    for mask, turn_ref in zip(masks, refs):
-        for side in range(2):
-            rows = rows_of(me ^ mask ^ (far * side), n)
-            out_ref[rows, :] = quick(turn_ref[side], mixed_ref[rows, :])
-
-
-def last_rows_kernel(masks, far, mixed_ref, *refs):
-    turn_refs, (_, out_ref, block_ref, sem_ref) = refs[:-4], refs[-4:]
+    turn_refs, (out_ref, block_ref, sem_ref) = refs[: len(masks)], refs[-3:]
     n = mixed_ref.shape[1]
     me = lax.axis_index("wide")
     copies = []
@@ -363,12 +355,11 @@
 
     one, two, tall = like(1, n, n), like(2, n, n), like(order_size, n)
     own = lax.dynamic_slice_in_dim(factor, me * n, n, 0)
-    cross = lax.dynamic_slice_in_dim(factor, (me ^ far) * n, n, 0)
     packed, qt, m = call(first_kernel, (like(n + n // 2, n), one, one), [], 2**32, own)
     packed = swap(packed, far)
     early = (swap(qt, far // 2), swap(qt, far // 2 | far)) if far > 1 else ()
     columns, right, moved = call(
-        columns_kernel, (tall, like(order_size // 2, n), like(n, n)), [], 2**28, factor, cross, qt
+        functools.partial(columns_kernel, far), (tall, like(order_size // 2, n), like(n, n)), [], 2**28, factor, qt
     )
     right = swap(right, far)
     scratch = [pltpu.VMEM((2, n, n), jnp.float32)] * 2
@@ -396,27 +387,26 @@
     pieces = spread_second(second, far, mixed)
     soon = [piece for piece in pieces if piece[0] < 2 or not piece[0] & 1]
     late = [piece for piece in pieces if piece[0] >= 2 and piece[0] & 1]
-    masks, held = zip(*soon)
-    rotated = call(functools.partial(rows_kernel, masks, far), tall, [], 2**29, mixed, *held)
-    if late:
-        masks, held = zip(*late)
-        anywhere = pl.BlockSpec(memory_space=pl.ANY)
-        inside = pl.BlockSpec(memory_space=pltpu.VMEM)
-        rotated = call(
-            functools.partial(last_rows_kernel, masks, far),
-            tall,
-            [
-                pltpu.VMEM((2 * len(late), n, n), jnp.float32),
-                pltpu.SemaphoreType.DMA((2 * len(late),)),
-            ],
-            2**29,
-            mixed,
-            *held,
-            rotated,
-            in_specs=[inside] * (1 + len(late)) + [anywhere],
-            out_specs=anywhere,
-            input_output_aliases={1 + len(late): 0},
-        )
+    rotated = ()
+    for part in (soon, late):
+        if part:
+            masks, held = zip(*part)
+            blocks = 2 * len(part)
+            rotated = call(
+                functools.partial(rows_kernel, masks, far),
+                tall,
+                [pltpu.VMEM((blocks, n, n), jnp.float32), pltpu.SemaphoreType.DMA((blocks,))],
+                2**29,
+                mixed,
+                *held,
+                *rotated,
+                in_specs=[pl.BlockSpec(memory_space=pltpu.VMEM)] * (1 + len(part))
+                + [pl.BlockSpec(memory_space=pl.ANY)] * len(rotated),
+                out_specs=pl.BlockSpec(memory_space=pl.ANY),
+                input_output_aliases={1 + len(part): 0} if rotated else {},
+            )
+            rotated = (rotated,)
+    (rotated,) = rotated
     return (rotated, eigen_basis)
 
 

time: 45.9 us -> 46 us (level)
  the two profiles are of different devices: /device:TPU:9 before, /device:TPU:25 now
where the time goes in v1:
time: 46 us; the launch traced here: 45.6 us
  starting transfers between devices  31.9 us (69%)
  Pallas kernels  11.5 us (25%)
  local copies, waits for them, and re-layouts  0.85 us (2%)
  between operations  0.69 us (2%)
  waiting for transfers between devices  0.65 us (1%)
    ppermute x10, starting transfers between devices, swap(): lax.ppermute(shard, 'wide', [(i, i ^ mask) for i in range(lax.axis_size('...  31.9 us
    pallas_call x7, Pallas kernels, call(): pl.pallas_call(kernel, out_shape=out_shape, scratch_shapes=scratch_shapes...  11.5 us
  transfers between devices with their start and end apart: 10, of which 1 were waited for; matrix products, arithmetic and copies ran while one was open for 0% of the time, Pallas kernels for 15%

profile of v1, /device:TPU:25, one launch (start us, length us, event | category | flops | bytes accessed | tf_op | source)
XLA Modules:
  0.0 45.6 jit_solution(11140348620274835334)
XLA Ops:
  0.6 0.8 %constant_dynamic-slice_fusion.own_ref = f32[128,128]{1,0:T(8,128)S(1)} fusion(f32[1024,128]{1,0:T(8,128)} %factor_ref.1, s32[]{:T(128)S(6)} %select_n.3), kind=kLoop, calls=%fused_computation | loop fusion | bytes 131076 | tf_op jit(solution)/shard_map/dynamic_slice | solution.py:357
  1.5 0.0 copy-start
  1.5 3.8 %shard_map.30 = (f32[192,128]{1,0:T(8,128)S(1)}, f32[1,128,128]{2,1,0:T(8,128)S(1)}, f32[1,128,128]{2,1,0:T(8,128)S(1)}) custom-call(f32[128,128]{1,0:T(8,128)S(1)} %constant_dynamic-slice_fusion.own_ref), custom_call_target="tpu_custom_call" | custom-call | flops 4294967296 | bytes 1048576 | tf_op jit(solution)/shard_map/pallas_call | solution.py:304
  5.3 24.8 %collective-permute-start = (f32[192,128]{1,0:T(8,128)S(1)}, f32[192,128]{1,0:T(8,128)S(1)}, u32[]{:S(2)}, u32[]{:S(2)}) collective-permute-start(f32[192,128]{1,0:T(8,128)S(1)} %get-tuple-element.19), channel_id=1, source_target_pairs={{0,16},{4,20},{8,24},{12,28},{16,0},{20,4},{24,8},{28,12},{1,17},{... | collective-permute-start | bytes 294920 | tf_op jit(solution)/shard_map/ppermute | solution.py:315
  30.2 1.2 %collective-permute-start.2 = (f32[1,128,128]{2,1,0:T(8,128)S(1)}, f32[1,128,128]{2,1,0:T(8,128)S(1)}, u32[]{:S(2)}, u32[]{:S(2)}) collective-permute-start(f32[1,128,128]{2,1,0:T(8,128)S(1)} %get-tuple-element.17.qt_ref.own_ref), channel_id=1, source_target_pairs={{0,8},{4,12},{8,0},{12,4},{16,24},{20,28},{24,16},{28,20},{1,9},{5... | collective-permute-start | bytes 196616 | tf_op jit(solution)/shard_map/ppermute | solution.py:315
  31.4 0.1 collective-permute-start.3
  31.4 0.0 copy-done
  31.4 0.5 %shard_map.31 = (f32[1024,128]{1,0:T(8,128)S(1)}, f32[512,128]{1,0:T(8,128)S(1)}, f32[128,128]{1,0:T(8,128)S(1)}) custom-call(f32[1024,128]{1,0:T(8,128)S(1)} %copy-done, f32[1,128,128]{2,1,0:T(8,128)S(1)} %get-tuple-element.17.qt_ref.own_ref), custom_call_target="tpu_custom_call" | custom-call | flops 268435456 | bytes 1048576 | tf_op jit(solution)/shard_map/pallas_call | solution.py:304
  31.9 1.5 %collective-permute-start.1 = (f32[512,128]{1,0:T(8,128)S(1)}, f32[512,128]{1,0:T(8,128)S(1)}, u32[]{:S(2)}, u32[]{:S(2)}) collective-permute-start(f32[512,128]{1,0:T(8,128)S(1)} %get-tuple-element.26), channel_id=1, source_target_pairs={{0,16},{4,20},{8,24},{12,28},{16,0},{20,4},{24,8},{28,12},{1,17},{... | collective-permute-start | bytes 786440 | tf_op jit(solution)/shard_map/ppermute | solution.py:315
  33.3 0.0 collective-permute-done.packed_ref
  33.3 3.6 %shard_map.32 = (f32[2,128,128]{2,1,0:T(8,128)S(1)}, f32[2,128,128]{2,1,0:T(8,128)S(1)}) custom-call(f32[192,128]{1,0:T(8,128)S(1)} %collective-permute-done.packed_ref, f32[1,128,128]{2,1,0:T(8,128)S(1)} %get-tuple-element.20.m_in_ref, f32[1,128,128]{2,1,0:T(8,128)S(1)} %get-tuple-element.17.qt_ref.own_ref, f32[128,128]{1,0:T(8,128)S(1)} %get-tuple-element.21.moved_ref), custom_call_target="tpu_custom_call" | custom-call | flops 17179869184 | bytes 1048576 | tf_op jit(solution)/shard_map/pallas_call | solution.py:304
  36.9 1.3 %collective-permute-start.7 = (f32[2,128,128]{2,1,0:T(8,128)S(1)}, f32[2,128,128]{2,1,0:T(8,128)S(1)}, u32[]{:S(2)}, u32[]{:S(2)}) collective-permute-start(f32[2,128,128]{2,1,0:T(8,128)S(1)} %get-tuple-element.22.second_ref.refs_0_), channel_id=1, source_target_pairs={{0,8},{4,12},{8,0},{12,4},{16,24},{20,28},{24,16},{28,20},{1,9},{5... | collective-permute-start | bytes 393224 | tf_op jit(solution)/shard_map/ppermute | solution.py:315
  38.2 0.7 %collective-permute-start.4 = (f32[2,128,128]{2,1,0:T(8,128)S(1)}, f32[2,128,128]{2,1,0:T(8,128)S(1)}, u32[]{:S(2)}, u32[]{:S(2)}) collective-permute-start(f32[2,128,128]{2,1,0:T(8,128)S(1)} %get-tuple-element.27.first_ref.refs_0_), channel_id=1, source_target_pairs={{0,4},{4,0},{8,12},{12,8},{16,20},{20,16},{24,28},{28,24},{1,5},{5... | collective-permute-start | bytes 393224 | tf_op jit(solution)/shard_map/ppermute | solution.py:315
  38.8 0.0 collective-permute-done.2.refs_1_
  38.8 0.1 collective-permute-start.5
  38.9 0.0 collective-permute-done.3.refs_2_
  38.9 0.4 collective-permute-start.6
  39.4 1.1 %shard_map.33 = (f32[1024,128]{1,0:T(8,128)S(1)}, f32[128,128]{1,0:T(8,128)S(1)}, f32[1024,128]{1,0:T(8,128)}) custom-call(f32[1024,128]{1,0:T(8,128)S(1)} %get-tuple-element.18.columns_ref, f32[2,128,128]{2,1,0:T(8,128)S(1)} %get-tuple-element.22.second_ref.refs_0_, f32[2,128,128]{2,1,0:T(8,128)S(1)} %get-tuple-element.27.first_ref.refs_0_), custom_call_target="tpu_custom_call" | custom-call | flops 2147483648 | bytes 1048576 | tf_op jit(solution)/shard_map/pallas_call | solution.py:304
  40.5 0.0 collective-permute-done.5.refs_4_
  40.5 0.1 collective-permute-start.9
  40.6 0.0 collective-permute-done.6.refs_5_
  40.6 0.0 collective-permute-done.4.refs_3_
  40.6 0.6 %collective-permute-done.1.right_ref = f32[512,128]{1,0:T(8,128)S(1)} collective-permute-done((f32[512,128]{1,0:T(8,128)S(1)}, f32[512,128]{1,0:T(8,128)S(1)}, u32[]{:S(2)}, u32[]{:S(2)}) %collective-permute-start.1) | collective-permute-done | bytes 262176 | tf_op jit(solution)/shard_map/ppermute | solution.py:315
  41.2 0.6 %shard_map.34.mixed_ref = f32[1024,128]{1,0:T(8,128)S(1)} custom-call(f32[1024,128]{1,0:T(8,128)S(1)} %get-tuple-element.24.turned_ref, f32[128,128]{1,0:T(8,128)S(1)} %get-tuple-element.25.turn_ref, f32[512,128]{1,0:T(8,128)S(1)} %collective-permute-done.1.right_ref, f32[2,128,128]{2,1,0:T(8,128)S(1)} %get-tuple-element.27.first_ref.refs_0_, ...), custom_call_target="tpu_custom_call" | custom-call | flops 2147483648 | bytes 1048576 | tf_op jit(solution)/shard_map/pallas_call | solution.py:304
  41.9 0.0 collective-permute-done.7.refs_1_
  41.9 1.9 %collective-permute-start.8 = (f32[2,128,128]{2,1,0:T(8,128)S(1)}, f32[2,128,128]{2,1,0:T(8,128)S(1)}, u32[]{:S(2)}, u32[]{:S(2)}) collective-permute-start(f32[2,128,128]{2,1,0:T(8,128)S(1)} %collective-permute-done.7.refs_1_), channel_id=1, source_target_pairs={{0,4},{4,0},{8,12},{12,8},{16,20},{20,16},{24,28},{28,24},{1,5},{5... | collective-permute-start | bytes 393224 | tf_op jit(solution)/shard_map/ppermute | solution.py:315
  43.7 0.0 collective-permute-done.9.refs_2_
  43.7 1.0 %shard_map.35.refs_1_ = f32[1024,128]{1,0:T(8,128)} custom-call(f32[1024,128]{1,0:T(8,128)S(1)} %shard_map.34.mixed_ref, f32[2,128,128]{2,1,0:T(8,128)S(1)} %get-tuple-element.22.second_ref.refs_0_, f32[2,128,128]{2,1,0:T(8,128)S(1)} %collective-permute-done.7.refs_1_, f32[2,128,128]{2,1,0:T(8,128)S(1)} %collective-permute-done.9.refs_2_), custom_call_target="tpu_custom_call" | custom-call | flops 536870912 | bytes 1048576 | tf_op jit(solution)/shard_map/pallas_call | solution.py:304
  44.7 0.0 collective-permute-done.8.refs_0_
  44.7 0.9 %shard_map.36 = f32[1024,128]{1,0:T(8,128)} custom-call(f32[1024,128]{1,0:T(8,128)S(1)} %shard_map.34.mixed_ref, f32[2,128,128]{2,1,0:T(8,128)S(1)} %collective-permute-done.8.refs_0_, f32[1024,128]{1,0:T(8,128)} %shard_map.35.refs_1_), custom_call_target="tpu_custom_call", output_to_operand_aliasing={{}: (2, {})} | custom-call | flops 536870912 | bytes 1048576 | tf_op jit(solution)/shard_map/pallas_call | solution.py:304
Async XLA Ops:
  1.5 29.9 %copy-start = (f32[1024,128]{1,0:T(8,128)S(1)}, f32[1024,128]{1,0:T(8,128)}, u32[]{:S(2)}) copy-start(f32[1024,128]{1,0:T(8,128)} %factor_ref.1) | copy-start | bytes 1572868
  5.3 28.0 %collective-permute-start = (f32[192,128]{1,0:T(8,128)S(1)}, f32[192,128]{1,0:T(8,128)S(1)}, u32[]{:S(2)}, u32[]{:S(2)}) collective-permute-start(f32[192,128]{1,0:T(8,128)S(1)} %get-tuple-element.19), channel_id=1, source_target_pairs={{0,16},{4,20},{8,24},{12,28},{16,0},{20,4},{24,8},{28,12},{1,17},{... | collective-permute-start | bytes 294920 | tf_op jit(solution)/shard_map/ppermute | solution.py:315
  30.2 8.7 %collective-permute-start.2 = (f32[1,128,128]{2,1,0:T(8,128)S(1)}, f32[1,128,128]{2,1,0:T(8,128)S(1)}, u32[]{:S(2)}, u32[]{:S(2)}) collective-permute-start(f32[1,128,128]{2,1,0:T(8,128)S(1)} %get-tuple-element.17.qt_ref.own_ref), channel_id=1, source_target_pairs={{0,8},{4,12},{8,0},{12,4},{16,24},{20,28},{24,16},{28,20},{1,9},{5... | collective-permute-start | bytes 196616 | tf_op jit(solution)/shard_map/ppermute | solution.py:315
  31.4 7.6 %collective-permute-start.3 = (f32[1,128,128]{2,1,0:T(8,128)S(1)}, f32[1,128,128]{2,1,0:T(8,128)S(1)}, u32[]{:S(2)}, u32[]{:S(2)}) collective-permute-start(f32[1,128,128]{2,1,0:T(8,128)S(1)} %get-tuple-element.17.qt_ref.own_ref), channel_id=1, source_target_pairs={{0,24},{4,28},{8,16},{12,20},{16,8},{20,12},{24,0},{28,4},{1,25},{... | collective-permute-start | bytes 196616 | tf_op jit(solution)/shard_map/ppermute | solution.py:315
  31.9 9.3 %collective-permute-start.1 = (f32[512,128]{1,0:T(8,128)S(1)}, f32[512,128]{1,0:T(8,128)S(1)}, u32[]{:S(2)}, u32[]{:S(2)}) collective-permute-start(f32[512,128]{1,0:T(8,128)S(1)} %get-tuple-element.26), channel_id=1, source_target_pairs={{0,16},{4,20},{8,24},{12,28},{16,0},{20,4},{24,8},{28,12},{1,17},{... | collective-permute-start | bytes 786440 | tf_op jit(solution)/shard_map/ppermute | solution.py:315
  36.9 5.0 %collective-permute-start.7 = (f32[2,128,128]{2,1,0:T(8,128)S(1)}, f32[2,128,128]{2,1,0:T(8,128)S(1)}, u32[]{:S(2)}, u32[]{:S(2)}) collective-permute-start(f32[2,128,128]{2,1,0:T(8,128)S(1)} %get-tuple-element.22.second_ref.refs_0_), channel_id=1, source_target_pairs={{0,8},{4,12},{8,0},{12,4},{16,24},{20,28},{24,16},{28,20},{1,9},{5... | collective-permute-start | bytes 393224 | tf_op jit(solution)/shard_map/ppermute | solution.py:315
  38.2 2.4 %collective-permute-start.4 = (f32[2,128,128]{2,1,0:T(8,128)S(1)}, f32[2,128,128]{2,1,0:T(8,128)S(1)}, u32[]{:S(2)}, u32[]{:S(2)}) collective-permute-start(f32[2,128,128]{2,1,0:T(8,128)S(1)} %get-tuple-element.27.first_ref.refs_0_), channel_id=1, source_target_pairs={{0,4},{4,0},{8,12},{12,8},{16,20},{20,16},{24,28},{28,24},{1,5},{5... | collective-permute-start | bytes 393224 | tf_op jit(solution)/shard_map/ppermute | solution.py:315
  38.8 1.7 %collective-permute-start.5 = (f32[1,128,128]{2,1,0:T(8,128)S(1)}, f32[1,128,128]{2,1,0:T(8,128)S(1)}, u32[]{:S(2)}, u32[]{:S(2)}) collective-permute-start(f32[1,128,128]{2,1,0:T(8,128)S(1)} %collective-permute-done.2.refs_1_), channel_id=1, source_target_pairs={{0,4},{4,0},{8,12},{12,8},{16,20},{20,16},{24,28},{28,24},{1,5},{5... | collective-permute-start | bytes 196616 | tf_op jit(solution)/shard_map/ppermute | solution.py:315
  38.9 1.6 %collective-permute-start.6 = (f32[1,128,128]{2,1,0:T(8,128)S(1)}, f32[1,128,128]{2,1,0:T(8,128)S(1)}, u32[]{:S(2)}, u32[]{:S(2)}) collective-permute-start(f32[1,128,128]{2,1,0:T(8,128)S(1)} %collective-permute-done.3.refs_2_), channel_id=1, source_target_pairs={{0,4},{4,0},{8,12},{12,8},{16,20},{20,16},{24,28},{28,24},{1,5},{5... | collective-permute-start | bytes 196616 | tf_op jit(solution)/shard_map/ppermute | solution.py:315
  40.5 3.2 %collective-permute-start.9 = (f32[2,128,128]{2,1,0:T(8,128)S(1)}, f32[2,128,128]{2,1,0:T(8,128)S(1)}, u32[]{:S(2)}, u32[]{:S(2)}) collective-permute-start(f32[2,128,128]{2,1,0:T(8,128)S(1)} %get-tuple-element.22.second_ref.refs_0_), channel_id=1, source_target_pairs={{0,4},{4,0},{8,12},{12,8},{16,20},{20,16},{24,28},{28,24},{1,5},{5... | collective-permute-start | bytes 393224 | tf_op jit(solution)/shard_map/ppermute | solution.py:315
  41.9 2.9 %collective-permute-start.8 = (f32[2,128,128]{2,1,0:T(8,128)S(1)}, f32[2,128,128]{2,1,0:T(8,128)S(1)}, u32[]{:S(2)}, u32[]{:S(2)}) collective-permute-start(f32[2,128,128]{2,1,0:T(8,128)S(1)} %collective-permute-done.7.refs_1_), channel_id=1, source_target_pairs={{0,4},{4,0},{8,12},{12,8},{16,20},{20,16},{24,28},{28,24},{1,5},{5... | collective-permute-start | bytes 393224 | tf_op jit(solution)/shard_map/ppermute | solution.py:315
